TPU v7x, 32 devices: a whole 2x2x4 slice. The times are simulated.
32 devices in a mesh: gx: 2 (over core), gy: 4 (over z), gz: 4 (over y, x).
Axes of the slice: x: 2, y: 2, z: 4, core: 2. Of those that a mesh axis runs over, the one named last changes fastest.
Arguments:
- cr_init: float32 [64, 16, 8, 512], P(None, 'gz', 'gx', 'gy'), may hold values from 0.1 to 3
- gas: float32 [16, 8, 512], P('gz', 'gx', 'gy'), may hold values from 0.05 to 3
- diff_coeff: float32 [64], replicated, may hold values from 0.06 to 0.14
- loss_coeff: float32 [64], replicated, may hold values from 0.05 to 0.3
- pi0_table: float32 [96, 64], replicated, may hold values from -0.75 to 0.75
- los_weight: bfloat16 [4, 2, 4, 7, 2048, 128], P('gz', 'gx', 'gy'), may hold values from -0.125 to 0.125
- slot_owner: int32 [4, 2, 4, 7, 1], P('gz', 'gx', 'gy'), may hold values from 0 to 3; in each aligned block of 7 rows (0 to 6, 7 to 13, ..., all dimensions but the last counted through in order) at most 3 rows name the same one
- slot_block: int32 [4, 2, 4, 7], P('gz', 'gx', 'gy'), may hold values from 0 to 3
Outputs:
- cr_final: float32 [64, 16, 8, 512], P(None, 'gz', 'gx', 'gy')
- sky: float32 [4, 2, 16, 96, 128], P('gz', 'gx', 'gy')
Inputs may be any that keep to these rules, and one draw needn't show every extreme that they name: `slot_owner`: at most 3 of the 7 weight blocks of one device name the same owner, and some device names one owner exactly 3 times.
All inputs are finite; a program needn't handle non-finite values.
Results may differ from a plain program's by a relative error of at most 0.0029.
Values sent between devices are 32-bit elements; how exact they have to be, the bound alone decides.
A program may use at most 64 MiB of HBM per device.

v0:
```python
import jax
import jax.numpy as jnp
from jax import lax
from jax.sharding import PartitionSpec as P

STEPS = 2
BO = 4


def extended(cells, sides, width):
    for axis, dim in sides:
        count = lax.axis_size(axis)
        ends = count - 1
        head = lax.slice_in_dim(cells, 0, width, axis=dim)
        tail = lax.slice_in_dim(cells, cells.shape[dim] - width, cells.shape[dim], axis=dim)
        cells = jnp.concatenate(
            [
                lax.ppermute(tail, axis, [(i, (i + 1) % count) for i in range(ends)]),
                cells,
                lax.ppermute(head, axis, [((i + 1) % count, i) for i in range(ends)]),
            ],
            axis=dim,
        )
    return cells


def advance(padded, diffusion, losses):
    center = padded[:, 1:-1, 1:-1, 1:-1]
    beside = padded[:, 2:, 1:-1, 1:-1] + padded[:, :-2, 1:-1, 1:-1]
    beside = beside + padded[:, 1:-1, 2:, 1:-1] + padded[:, 1:-1, :-2, 1:-1]
    beside = beside + padded[:, 1:-1, 1:-1, 2:] + padded[:, 1:-1, 1:-1, :-2]
    loss_flux = losses[:, None, None, None] * center
    from_above = jnp.concatenate([loss_flux[1:], jnp.zeros_like(loss_flux[:1])], axis=0)
    return (
        center + diffusion[:, None, None, None] * (beside - 6.0 * center) + from_above - loss_flux
    )


def body(cr_init, gas, diff_coeff, loss_coeff, pi0_table, los_weight, slot_owner, slot_block):
    density = cr_init
    for step_index in range(STEPS):
        padded = extended(density, (("gx", 2), ("gy", 3), ("gz", 1)), 1)
        density = advance(padded, diff_coeff, loss_coeff)
    source = jnp.einsum("ge,ezxy->gzxy", pi0_table, density, precision=lax.Precision.HIGHEST)
    emissivity = (gas[None] * source).astype(jnp.bfloat16)
    flat_cells = emissivity.reshape(emissivity.shape[0], -1)
    weights = los_weight[0, 0, 0]
    contrib = jnp.einsum("gc,scp->sgp", flat_cells, weights, preferred_element_type=jnp.float32)
    gamma_count = contrib.shape[1]
    pixel_count = contrib.shape[2]
    owners = slot_owner[0, 0, 0, :, 0]
    blocks = slot_block[0, 0, 0]
    owner_count = lax.axis_size("gy")
    target = owners * BO + blocks
    select = (target[None, :] == jnp.arange(owner_count * BO)[:, None]).astype(jnp.float32)
    terms = jnp.einsum("rs,sgp->rgp", select, contrib, precision=lax.Precision.HIGHEST)
    sky = lax.psum_scatter(terms, "gy", scatter_dimension=0, tiled=True)
    return (density, sky.reshape(1, 1, BO, gamma_count, pixel_count))


def solution(mesh):
    in_specs = (
        P(None, "gz", "gx", "gy"),
        P("gz", "gx", "gy"),
        P(),
        P(),
        P(),
        P("gz", "gx", "gy", None, None, None),
        P("gz", "gx", "gy", None, None),
        P("gz", "gx", "gy", None),
    )
    out_specs = (P(None, "gz", "gx", "gy"), P("gz", "gx", "gy", None, None))
    return jax.shard_map(body, mesh=mesh, in_specs=in_specs, out_specs=out_specs, check_vma=False)
```

profile of v0, /device:TPU:0, one launch (start us, length us, event | category | flops | bytes accessed | tf_op | source)
XLA Modules:
  0.0 132.2 jit_solution(6889490880163219519)
XLA Ops:
  7.2 0.0 copy-start
  7.2 0.0 reduce-scatter.2.cloned.1.call-start
  7.2 1.4 %copy.38 = f32[64,4,4,128]{0,1,3,2:T(4,128)S(1)} copy(f32[64,4,4,128]{3,2,1,0:T(4,128)} %param.8) | data formatting | bytes 1048576 | tf_op args[0]
  8.7 0.0 copy-start.3
  8.7 2.4 %collective-permute-start = (f32[64,4,1,128]{0,1,3,2:T(4,128)S(1)}, f32[64,4,1,128]{0,1,3,2:T(4,128)S(1)}, u32[]{:S(2)}, u32[]{:S(2)}) collective-permute-start(f32[64,4,1,128]{0,1,3,2:T(4,128)S(1)} %get-tuple-element.22), channel_id=1, source_target_pairs={{0,16},{1,17},{2,18},{3,19},{4,20},{5,21},{6,22},{7,23},{8,24},{9,... | collective-permute-start | bytes 393224 | tf_op jit(solution)/shard_map/ppermute | solution.py:18
  11.1 1.3 collective-permute-start.1
  12.4 0.0 collective-permute-done
  12.4 2.1 %collective-permute-done.1 = f32[64,4,1,128]{0,1,3,2:T(4,128)S(1)} collective-permute-done((f32[64,4,1,128]{0,1,3,2:T(4,128)S(1)}, f32[64,4,1,128]{0,1,3,2:T(4,128)S(1)}, u32[]{:S(2)}, u32[]{:S(2)}) %collective-permute-start.1) | collective-permute-done | bytes 131104 | tf_op jit(solution)/shard_map/ppermute | solution.py:20
  14.5 0.0 copy-start.1
  14.6 4.3 %collective-permute-start.2 = (f32[64,4,6,1]{0,1,3,2:T(4,128)S(1)}, f32[64,4,6,1]{0,1,3,2:T(4,128)S(1)}, u32[]{:S(2)}, u32[]{:S(2)}) collective-permute-start(f32[64,4,6,1]{0,1,3,2:T(4,128)S(1)} %get-tuple-element.19), channel_id=1, source_target_pairs={{0,4},{4,8},{8,12},{1,5},{5,9},{9,13},{2,6},{6,10},{10,14},{3,7},{... | collective-permute-start | bytes 18440 | tf_op jit(solution)/shard_map/ppermute | solution.py:18
  18.9 1.3 collective-permute-start.3
  20.2 0.1 collective-permute-done.2
  20.3 4.2 %collective-permute-done.3 = f32[64,4,6,1]{0,1,3,2:T(4,128)S(1)} collective-permute-done((f32[64,4,6,1]{0,1,3,2:T(4,128)S(1)}, f32[64,4,6,1]{0,1,3,2:T(4,128)S(1)}, u32[]{:S(2)}, u32[]{:S(2)}) %collective-permute-start.3) | collective-permute-done | bytes 6176 | tf_op jit(solution)/shard_map/ppermute | solution.py:20
  24.5 1.3 %pad_maximum_fusion.45 = (f32[64,1,6,130]{0,1,3,2:T(1,128)S(1)}, f32[64,1,6,130]{0,1,3,2:T(1,128)S(1)}) fusion(f32[64,4,6,1]{0,1,3,2:T(4,128)S(1)} %collective-permute-done.3, f32[64,4,6,1]{0,1,3,2:T(4,128)S(1)} %collective-permute-done.2, f32[64,4,1,128]{0,1,3,2:T(4,128)S(1)} %collective-permute-done.1, f32[64,4,4,128]{0,1,3,2:T(4,128)S(1)} %copy.38, ...), kind=kLoop, calls=%fused_computation.74 | loop fusion | flops 399360 | bytes 1198080 | tf_op jit(solution)/shard_map/slice | solution.py:14
  25.8 0.0 copy-start.4
  25.8 0.4 copy.31
  26.2 1.3 collective-permute-start.4
  27.5 1.1 copy.33
  28.6 4.6 %collective-permute-start.5 = (f32[64,1,6,130]{3,0,2,1:T(8,128)}, f32[64,1,6,130]{3,0,2,1:T(8,128)S(1)}, u32[]{:S(2)}, u32[]{:S(2)}) collective-permute-start(f32[64,1,6,130]{3,0,2,1:T(8,128)} %copy.33), channel_id=1, source_target_pairs={{0,1},{1,2},{2,3},{4,5},{5,6},{6,7},{8,9},{9,10},{10,11},{12,13},{... | collective-permute-start | bytes 599048 | tf_op jit(solution)/shard_map/ppermute | solution.py:18
  33.2 0.0 copy-done.3
  33.2 0.2 broadcast_multiply_fusion.1
  33.4 0.0 copy-done.1
  33.4 1.6 %slice.118 = f32[63,4,4,128]{0,1,3,2:T(4,128)} slice(f32[64,4,4,128]{0,1,3,2:T(4,128)S(1)} %broadcast_multiply_fusion.1), slice={[1:64], [0:4], [0:4], [0:128]} | slice | bytes 1032192 | tf_op jit(solution)/shard_map/slice | solution.py:33
  35.0 5.2 %collective-permute-done.4 = f32[64,1,6,130]{3,0,2,1:T(8,128)S(1)} collective-permute-done((f32[64,1,6,130]{3,0,2,1:T(8,128)S(1)}, f32[64,1,6,130]{3,0,2,1:T(8,128)S(1)}, u32[]{:S(2)}, u32[]{:S(2)}) %collective-permute-start.4) | collective-permute-done | bytes 199712 | tf_op jit(solution)/shard_map/ppermute | solution.py:20
  40.2 1.1 copy.32
  41.3 0.0 collective-permute-done.5
  41.3 1.1 copy.34
  42.3 0.0 copy-done.4
  42.3 5.5 %broadcast_multiply_fusion = (f32[64,4,4,128]{0,1,3,2:T(4,128)S(1)}, f32[64,4,4,128]{0,1,3,2:T(4,128)S(1)}) fusion(f32[64]{0:T(128)S(1)} %copy-done.3, f32[64,4,4,128]{0,1,3,2:T(4,128)S(1)} %copy.38, f32[63,4,4,128]{0,1,3,2:T(4,128)} %slice.118, f32[64,4,1,128]{0,1,3,2:T(4,128)} %copy-done.1, f32[64,4,1,128]{0,1,3,2:T(4,128)S(1)} %collective-permute-done, ...), kind=kLoop, calls=%fused_computation.63 | loop fusion | flops 4063232 | bytes 2763264 | tf_op jit(solution)/shard_map/mul | solution.py:32
  47.9 0.0 copy-start.5
  47.9 0.0 copy-start.6
  48.0 1.3 collective-permute-start.6
  49.3 1.3 collective-permute-start.7
  50.6 0.0 collective-permute-done.6
  50.6 2.1 %collective-permute-done.7 = f32[64,4,1,128]{0,1,3,2:T(4,128)S(1)} collective-permute-done((f32[64,4,1,128]{0,1,3,2:T(4,128)S(1)}, f32[64,4,1,128]{0,1,3,2:T(4,128)S(1)}, u32[]{:S(2)}, u32[]{:S(2)}) %collective-permute-start.7) | collective-permute-done | bytes 131104 | tf_op jit(solution)/shard_map/ppermute | solution.py:20
  52.7 3.5 %collective-permute-start.8 = (f32[64,4,6,1]{0,1,3,2:T(4,128)S(1)}, f32[64,4,6,1]{0,1,3,2:T(4,128)S(1)}, u32[]{:S(2)}, u32[]{:S(2)}) collective-permute-start(f32[64,4,6,1]{0,1,3,2:T(4,128)S(1)} %get-tuple-element.17), channel_id=1, source_target_pairs={{0,4},{4,8},{8,12},{1,5},{5,9},{9,13},{2,6},{6,10},{10,14},{3,7},{... | collective-permute-start | bytes 18440 | tf_op jit(solution)/shard_map/ppermute | solution.py:18
  56.2 1.3 collective-permute-start.9
  57.5 0.1 collective-permute-done.8
  57.6 4.2 %collective-permute-done.9 = f32[64,4,6,1]{0,1,3,2:T(4,128)S(1)} collective-permute-done((f32[64,4,6,1]{0,1,3,2:T(4,128)S(1)}, f32[64,4,6,1]{0,1,3,2:T(4,128)S(1)}, u32[]{:S(2)}, u32[]{:S(2)}) %collective-permute-start.9) | collective-permute-done | bytes 6176 | tf_op jit(solution)/shard_map/ppermute | solution.py:20
  61.8 2.0 %pad_maximum_fusion.40 = (f32[64,1,6,130]{0,1,3,2:T(1,128)}, f32[64,1,6,130]{0,1,3,2:T(1,128)S(1)}) fusion(f32[64,4,6,1]{0,1,3,2:T(4,128)S(1)} %collective-permute-done.9, f32[64,4,6,1]{0,1,3,2:T(4,128)S(1)} %collective-permute-done.8, f32[64,4,1,128]{0,1,3,2:T(4,128)S(1)} %collective-permute-done.7, f32[64,4,4,128]{0,1,3,2:T(4,128)S(1)} %get-tuple-element.11, ...), kind=kLoop, calls=%fused_computation.69 | loop fusion | flops 399360 | bytes 1198080 | tf_op jit(solution)/shard_map/slice | solution.py:14
  63.8 1.9 %copy.40 = f32[64,1,6,130]{3,0,2,1:T(8,128)} copy(f32[64,1,6,130]{0,1,3,2:T(1,128)} %get-tuple-element.12) | data formatting | bytes 399360 | tf_op jit(solution)/shard_map/slice | solution.py:14
  65.7 1.3 collective-permute-start.10
  67.0 1.1 copy.42
  68.1 7.2 %collective-permute-start.11 = (f32[64,1,6,130]{3,0,2,1:T(8,128)}, f32[64,1,6,130]{3,0,2,1:T(8,128)S(1)}, u32[]{:S(2)}, u32[]{:S(2)}) collective-permute-start(f32[64,1,6,130]{3,0,2,1:T(8,128)} %copy.42), channel_id=1, source_target_pairs={{0,1},{1,2},{2,3},{4,5},{5,6},{6,7},{8,9},{9,10},{10,11},{12,13},{... | collective-permute-start | bytes 599048 | tf_op jit(solution)/shard_map/ppermute | solution.py:18
  75.3 0.0 copy-done.5
  75.3 0.0 copy-done.6
  75.3 0.0 copy-start.2
  75.4 1.6 %slice.121 = f32[63,4,4,128]{0,1,3,2:T(4,128)} slice(f32[64,4,4,128]{0,1,3,2:T(4,128)S(1)} %get-tuple-element.10), slice={[1:64], [0:4], [0:4], [0:128]} | slice | bytes 1032192 | tf_op jit(solution)/shard_map/slice | solution.py:33
  77.0 5.7 %collective-permute-done.10 = f32[64,1,6,130]{3,0,2,1:T(8,128)} collective-permute-done((f32[64,1,6,130]{3,0,2,1:T(8,128)}, f32[64,1,6,130]{3,0,2,1:T(8,128)}, u32[]{:S(2)}, u32[]{:S(2)}) %collective-permute-start.10) | collective-permute-done | bytes 199712 | tf_op jit(solution)/shard_map/ppermute | solution.py:20
  82.7 1.3 %copy.41 = f32[64,1,6,130]{0,1,3,2:T(1,128)S(1)} copy(f32[64,1,6,130]{3,0,2,1:T(8,128)} %collective-permute-done.10) | data formatting | bytes 399360 | tf_op jit(solution)/shard_map/ppermute | solution.py:20
  84.0 0.0 collective-permute-done.11
  84.0 1.1 copy.43
  85.1 5.4 %fusion.12 = f32[64,4,4,128]{0,1,3,2:T(4,128)S(1)} fusion(f32[64,4,4,128]{0,1,3,2:T(4,128)S(1)} %get-tuple-element.11, f32[64,4,6,1]{0,1,3,2:T(4,128)S(1)} %collective-permute-done.8, f32[64,4,1,128]{0,1,3,2:T(4,128)S(1)} %collective-permute-done.7, f32[64,4,1,128]{0,1,3,2:T(4,128)S(1)} %collective-permute-done.6, ...), kind=kLoop, calls=%fused_computation.12 | loop fusion | flops 3932160 | bytes 2238976 | tf_op jit(solution)/shard_map/sub | solution.py:35
  90.5 0.0 copy-done
  90.5 0.0 copy-done.2
  90.6 1.2 fusion.3
  91.8 0.2 copy.45
  92.0 0.3 reshape.28
  92.3 2.7 %fusion.4 = f32[7,96,128]{2,1,0:T(8,128)S(1)} fusion(bf16[96,2048,1]{1,0,2:T(8,128)(2,1)S(1)} %reshape.28, bf16[1,1,1,7,2048,128]{5,4,3,2,1,0:T(8,128)(2,1)} %param.13), kind=kOutput, calls=%fused_computation.5 | convolution fusion | flops 352321536 | bytes 4407296 | tf_op jit(solution)/shard_map/gc,scp->sgp/dot_general | solution.py:48
  95.0 0.7 fusion.28
  95.8 1.1 copy.47
  96.9 0.0 reduce-scatter.2.cloned.1.call-update
  97.0 1.2 copy.48
  98.1 27.3 %reduce-scatter.2.cloned.1.call-done = f32[4,96,128]{2,1,0:T(8,128)} async-done(((f32[16,96,128]{2,1,0:T(8,128)}), f32[4,96,128]{2,1,0:T(8,128)}) %reduce-scatter.2.cloned.1.call-update) | async-done | bytes 196624 | tf_op jit(solution)/shard_map/reduce_scatter | solution.py:57
  (5 shorter events, 0.1 us)
Async XLA Ops:
  7.2 83.4 %copy-start = (f32[96,64]{0,1:T(8,128)S(1)}, f32[96,64]{0,1:T(8,128)}, u32[]{:S(2)}) copy-start(f32[96,64]{0,1:T(8,128)} %param.12) | copy-start | bytes 73732
  7.2 118.2 %reduce-scatter.2.cloned.1.call-start = ((), (), s32[]{:S(2)}) async-start(), calls=%async_computation.1 | async-start | bytes 983040 | tf_op jit(solution)/shard_map/reduce_scatter | solution.py:57
  8.7 24.5 %copy-start.3 = (f32[64]{0:T(128)S(1)}, f32[64]{0:T(128)}, u32[]{:S(2)}) copy-start(f32[64]{0:T(128)} %param.11) | copy-start | bytes 772
  8.7 3.7 %collective-permute-start = (f32[64,4,1,128]{0,1,3,2:T(4,128)S(1)}, f32[64,4,1,128]{0,1,3,2:T(4,128)S(1)}, u32[]{:S(2)}, u32[]{:S(2)}) collective-permute-start(f32[64,4,1,128]{0,1,3,2:T(4,128)S(1)} %get-tuple-element.22), channel_id=1, source_target_pairs={{0,16},{1,17},{2,18},{3,19},{4,20},{5,21},{6,22},{7,23},{8,24},{9,... | collective-permute-start | bytes 393224 | tf_op jit(solution)/shard_map/ppermute | solution.py:18
  11.1 3.4 %collective-permute-start.1 = (f32[64,4,1,128]{0,1,3,2:T(4,128)S(1)}, f32[64,4,1,128]{0,1,3,2:T(4,128)S(1)}, u32[]{:S(2)}, u32[]{:S(2)}) collective-permute-start(f32[64,4,1,128]{0,1,3,2:T(4,128)S(1)} %get-tuple-element.23), channel_id=1, source_target_pairs={{16,0},{17,1},{18,2},{19,3},{20,4},{21,5},{22,6},{23,7},{24,8},{25... | collective-permute-start | bytes 393224 | tf_op jit(solution)/shard_map/ppermute | solution.py:20
  14.5 18.8 %copy-start.1 = (f32[64,4,1,128]{0,1,3,2:T(4,128)}, f32[64,4,1,128]{0,1,3,2:T(4,128)S(1)}, u32[]{:S(2)}) copy-start(f32[64,4,1,128]{0,1,3,2:T(4,128)S(1)} %collective-permute-done.1) | copy-start | bytes 393220
  14.6 5.7 %collective-permute-start.2 = (f32[64,4,6,1]{0,1,3,2:T(4,128)S(1)}, f32[64,4,6,1]{0,1,3,2:T(4,128)S(1)}, u32[]{:S(2)}, u32[]{:S(2)}) collective-permute-start(f32[64,4,6,1]{0,1,3,2:T(4,128)S(1)} %get-tuple-element.19), channel_id=1, source_target_pairs={{0,4},{4,8},{8,12},{1,5},{5,9},{9,13},{2,6},{6,10},{10,14},{3,7},{... | collective-permute-start | bytes 18440 | tf_op jit(solution)/shard_map/ppermute | solution.py:18
  18.9 5.6 %collective-permute-start.3 = (f32[64,4,6,1]{0,1,3,2:T(4,128)S(1)}, f32[64,4,6,1]{0,1,3,2:T(4,128)S(1)}, u32[]{:S(2)}, u32[]{:S(2)}) collective-permute-start(f32[64,4,6,1]{0,1,3,2:T(4,128)S(1)} %get-tuple-element.18), channel_id=1, source_target_pairs={{4,0},{8,4},{12,8},{5,1},{9,5},{13,9},{6,2},{10,6},{14,10},{7,3},{... | collective-permute-start | bytes 18440 | tf_op jit(solution)/shard_map/ppermute | solution.py:20
  25.8 16.5 %copy-start.4 = (f32[64]{0:T(128)S(1)}, f32[64]{0:T(128)}, u32[]{:S(2)}) copy-start(f32[64]{0:T(128)} %param.10) | copy-start | bytes 772
  26.2 13.9 %collective-permute-start.4 = (f32[64,1,6,130]{3,0,2,1:T(8,128)S(1)}, f32[64,1,6,130]{3,0,2,1:T(8,128)S(1)}, u32[]{:S(2)}, u32[]{:S(2)}) collective-permute-start(f32[64,1,6,130]{3,0,2,1:T(8,128)S(1)} %copy.31), channel_id=1, source_target_pairs={{1,0},{2,1},{3,2},{5,4},{6,5},{7,6},{9,8},{10,9},{11,10},{13,12},{... | collective-permute-start | bytes 599048 | tf_op jit(solution)/shard_map/ppermute | solution.py:20
  28.6 12.7 %collective-permute-start.5 = (f32[64,1,6,130]{3,0,2,1:T(8,128)}, f32[64,1,6,130]{3,0,2,1:T(8,128)S(1)}, u32[]{:S(2)}, u32[]{:S(2)}) collective-permute-start(f32[64,1,6,130]{3,0,2,1:T(8,128)} %copy.33), channel_id=1, source_target_pairs={{0,1},{1,2},{2,3},{4,5},{5,6},{6,7},{8,9},{9,10},{10,11},{12,13},{... | collective-permute-start | bytes 599048 | tf_op jit(solution)/shard_map/ppermute | solution.py:18
  47.9 27.4 %copy-start.5 = (s32[1,1,1,7]{3,2,1,0:T(1,128)S(1)}, s32[1,1,1,7]{3,2,1,0:T(1,128)}, u32[]{:S(2)}) copy-start(s32[1,1,1,7]{3,2,1,0:T(1,128)} %param.15) | copy-start | bytes 88
  47.9 27.4 %copy-start.6 = (s32[1,1,1,7,1]{3,4,2,1,0:T(1,128)S(1)}, s32[1,1,1,7,1]{3,4,2,1,0:T(1,128)}, u32[]{:S(2)}) copy-start(s32[1,1,1,7,1]{3,4,2,1,0:T(1,128)} %param.14) | copy-start | bytes 88
  48.0 2.6 %collective-permute-start.6 = (f32[64,4,1,128]{0,1,3,2:T(4,128)S(1)}, f32[64,4,1,128]{0,1,3,2:T(4,128)S(1)}, u32[]{:S(2)}, u32[]{:S(2)}) collective-permute-start(f32[64,4,1,128]{0,1,3,2:T(4,128)S(1)} %get-tuple-element.20), channel_id=1, source_target_pairs={{0,16},{1,17},{2,18},{3,19},{4,20},{5,21},{6,22},{7,23},{8,24},{9,... | collective-permute-start | bytes 393224 | tf_op jit(solution)/shard_map/ppermute | solution.py:18
  49.3 3.4 %collective-permute-start.7 = (f32[64,4,1,128]{0,1,3,2:T(4,128)S(1)}, f32[64,4,1,128]{0,1,3,2:T(4,128)S(1)}, u32[]{:S(2)}, u32[]{:S(2)}) collective-permute-start(f32[64,4,1,128]{0,1,3,2:T(4,128)S(1)} %get-tuple-element.21), channel_id=1, source_target_pairs={{16,0},{17,1},{18,2},{19,3},{20,4},{21,5},{22,6},{23,7},{24,8},{25... | collective-permute-start | bytes 393224 | tf_op jit(solution)/shard_map/ppermute | solution.py:20
  52.7 4.9 %collective-permute-start.8 = (f32[64,4,6,1]{0,1,3,2:T(4,128)S(1)}, f32[64,4,6,1]{0,1,3,2:T(4,128)S(1)}, u32[]{:S(2)}, u32[]{:S(2)}) collective-permute-start(f32[64,4,6,1]{0,1,3,2:T(4,128)S(1)} %get-tuple-element.17), channel_id=1, source_target_pairs={{0,4},{4,8},{8,12},{1,5},{5,9},{9,13},{2,6},{6,10},{10,14},{3,7},{... | collective-permute-start | bytes 18440 | tf_op jit(solution)/shard_map/ppermute | solution.py:18
  56.2 5.6 %collective-permute-start.9 = (f32[64,4,6,1]{0,1,3,2:T(4,128)S(1)}, f32[64,4,6,1]{0,1,3,2:T(4,128)S(1)}, u32[]{:S(2)}, u32[]{:S(2)}) collective-permute-start(f32[64,4,6,1]{0,1,3,2:T(4,128)S(1)} %get-tuple-element.16), channel_id=1, source_target_pairs={{4,0},{8,4},{12,8},{5,1},{9,5},{13,9},{6,2},{10,6},{14,10},{7,3},{... | collective-permute-start | bytes 18440 | tf_op jit(solution)/shard_map/ppermute | solution.py:20
  65.7 16.9 %collective-permute-start.10 = (f32[64,1,6,130]{3,0,2,1:T(8,128)}, f32[64,1,6,130]{3,0,2,1:T(8,128)}, u32[]{:S(2)}, u32[]{:S(2)}) collective-permute-start(f32[64,1,6,130]{3,0,2,1:T(8,128)} %copy.40), channel_id=1, source_target_pairs={{1,0},{2,1},{3,2},{5,4},{6,5},{7,6},{9,8},{10,9},{11,10},{13,12},{... | collective-permute-start | bytes 599048 | tf_op jit(solution)/shard_map/ppermute | solution.py:20
  68.1 15.9 %collective-permute-start.11 = (f32[64,1,6,130]{3,0,2,1:T(8,128)}, f32[64,1,6,130]{3,0,2,1:T(8,128)S(1)}, u32[]{:S(2)}, u32[]{:S(2)}) collective-permute-start(f32[64,1,6,130]{3,0,2,1:T(8,128)} %copy.42), channel_id=1, source_target_pairs={{0,1},{1,2},{2,3},{4,5},{5,6},{6,7},{8,9},{9,10},{10,11},{12,13},{... | collective-permute-start | bytes 599048 | tf_op jit(solution)/shard_map/ppermute | solution.py:18
  75.3 15.2 %copy-start.2 = (f32[4,4,128]{2,1,0:T(4,128)S(1)}, f32[4,4,128]{2,1,0:T(4,128)}, u32[]{:S(2)}) copy-start(f32[4,4,128]{2,1,0:T(4,128)} %param.9) | copy-start | bytes 24580
Sparse Core Ops, SparseCore 0:
  97.1 28.2 reduce-scatter.1
where the time goes:
time: 133 us; the launch traced here: 132 us
  waiting for transfers between devices  51 us (38%)
  starting transfers between devices  31 us (23%)
  local copies, waits for them, and re-layouts  16.6 us (12%)
  other arithmetic  14.5 us (11%)
  between operations  14.4 us (11%)
  matrix products  4.73 us (4%)
    reduce_scatter x1, waiting for transfers between devices, body(): sky = lax.psum_scatter(terms, 'gy', scatter_dimension=0, tiled=True)  27.3 us
    ppermute x6, waiting for transfers between devices, extended(): lax.ppermute(head, axis, [((i + 1) % count, i) for i in range(ends)])  23.5 us
    ppermute x6, starting transfers between devices, extended(): lax.ppermute(tail, axis, [(i, (i + 1) % count) for i in range(ends)])  23.2 us
    ppermute x6, starting transfers between devices, extended(): lax.ppermute(head, axis, [((i + 1) % count, i) for i in range(ends)])  7.74 us
    mul x2, other arithmetic, advance(): loss_flux = losses[:, None, None, None] * center  5.71 us
    sub x1, other arithmetic, advance(): center + diffusion[:, None, None, None] * (beside - 6.0 * center)  5.43 us
    slice x2, other arithmetic, extended(): head = lax.slice_in_dim(cells, 0, width, axis=dim)  3.36 us
    slice x2, local copies, waits for them, and re-layouts, advance(): loss_flux[1:]  3.25 us
  transfers between devices with their start and end apart: 13, of which 9 were waited for; matrix products, arithmetic and copies ran while one was open for 7% of the time, Pallas kernels for 0%

commit v1 on v0

v1 whole, which is shorter than its diff:
```python
import functools

import jax
import jax.numpy as jnp
from jax import lax
from jax.experimental import pallas as pl
from jax.experimental.pallas import tpu as pltpu
from jax.sharding import PartitionSpec as P

BO = 4
CAP = 3
CHUNKS = 4
PAD = 8
MESH = pl.DeviceIdType.MESH


def kernel(
    sizes, cr_ref, gas_ref, diff_ref, loss_ref, pi0_ref, owner_ref, block_ref, weight_hbm,
    out_ref, sky_ref,
    first, second, halo_z, halo_x, halo_y, pack, coef, weights, lhs, contrib, slots, landed,
    names, landed_names,
    weight_sem, halo_send, halo_recv, sky_send, sky_recv, name_send, name_recv,
):
    nx, ny, nz = sizes
    energies = diff_ref.shape[1]
    cz, cx = first.shape[0], first.shape[1]
    lanes = first.shape[3]
    cells = cz * cx
    size = energies // CHUNKS
    slot_count = weights.shape[0]
    gx, gy, gz = lax.axis_index("gx"), lax.axis_index("gy"), lax.axis_index("gz")

    load = pltpu.make_async_copy(weight_hbm, weights, weight_sem)
    load.start()

    exists = (gz > 0, gz < nz - 1, gx > 0, gx < nx - 1, gy > 0, gy < ny - 1)
    places = (
        (gx, gy, gz - 1), (gx, gy, gz + 1), (gx - 1, gy, gz), (gx + 1, gy, gz),
        (gx, gy - 1, gz), (gx, gy + 1, gz),
    )

    barrier = pltpu.get_barrier_semaphore()
    for side in range(4):
        @pl.when(exists[side])
        def _(side=side):
            pl.semaphore_signal(barrier, inc=1, device_id=places[side], device_id_type=MESH)
    for offset in range(1, ny):
        pl.semaphore_signal(
            barrier, inc=1, device_id=(gx, lax.rem(gy + offset, ny), gz), device_id_type=MESH
        )

    for cell in range(cells):
        first[cell // cx, cell % cx, 0:energies, :] = cr_ref[pl.ds(cell, energies, stride=cells), :]
    first[:, :, energies:, :] = jnp.zeros((cz, cx, PAD, lanes), jnp.float32)
    second[:, :, energies:, :] = jnp.zeros((cz, cx, PAD, lanes), jnp.float32)

    row = lax.broadcasted_iota(jnp.int32, (energies, energies), 0)
    column = lax.broadcasted_iota(jnp.int32, (energies, energies), 1)
    diff = jnp.broadcast_to(diff_ref[...], (energies, energies))
    loss = jnp.broadcast_to(loss_ref[...], (energies, energies))
    for index, (values, mask) in enumerate(
        ((diff, row == column), (loss, row == column), (loss, row + 1 == column))
    ):
        spread = jnp.sum(jnp.where(mask, values, 0.0), axis=1, keepdims=True)
        coef[index] = jnp.broadcast_to(spread, (energies, lanes))

    for side in range(6):
        @pl.when(jnp.logical_not(exists[side]))
        def _(side=side):
            halo = (halo_z, halo_x, halo_y)[side // 2]
            for step in range(2):
                halo[step, side % 2] = jnp.zeros(halo.shape[2:], jnp.float32)

    lane = lax.broadcasted_iota(jnp.int32, (size, lanes), 1)
    rows_of = [pl.ds(energies - size * (c + 1), size) for c in range(CHUNKS)]

    def halo_copy(step, chunk, side, arriving):
        rows = rows_of[chunk]
        source = (first, second)[step]
        far = side % 2 == 1
        if side < 2:
            src = source.at[cz - 1 if far else 0, :, rows, :]
        elif side < 4:
            src = source.at[:, cx - 1 if far else 0, rows, :]
        else:
            src = pack.at[step, rows, :]
        halo = (halo_z, halo_x, halo_y)[side // 2]
        lands = side % 2 if arriving else 1 - side % 2
        sem_side = side if arriving else side ^ 1
        if side < 4:
            dst = halo.at[step, lands, :, rows, :]
        else:
            dst = halo.at[step, lands, rows, :]
        return pltpu.make_async_remote_copy(
            src_ref=src, dst_ref=dst,
            send_sem=halo_send.at[step, chunk, side],
            recv_sem=halo_recv.at[step, chunk, sem_side],
            device_id=places[side], device_id_type=MESH,
        )

    def pack_rows(step, chunk):
        source = (first, second)[step]
        packed = jnp.zeros((size, lanes), jnp.float32)
        for cell in range(cells):
            turned = pltpu.roll(source[cell // cx, cell % cx, rows_of[chunk], :], 2 * cell + 1, 1)
            packed = jnp.where(lane // 2 == cell, turned, packed)
        pack[step, rows_of[chunk], :] = packed

    def send_halos(step, chunk):
        for side in range(6):
            @pl.when(exists[side])
            def _(side=side):
                halo_copy(step, chunk, side, False).start()

    def wait_halos(step, chunk):
        for side in range(6):
            @pl.when(exists[side])
            def _(side=side):
                halo_copy(step, chunk, side, True).wait_recv()

    def advance(step, chunk, emit):
        source = (first, second)[step]
        rows = rows_of[chunk]
        above_rows = pl.ds(energies - size * (chunk + 1) + 1, size)
        diffusion, losses, losses_above = coef[0, rows, :], coef[1, rows, :], coef[2, rows, :]
        left = pltpu.roll(halo_y[step, 0, rows, :], 1, 1)
        right = pltpu.roll(halo_y[step, 1, rows, :], lanes - 1, 1)
        faces = jnp.where(lane % 2 == 1, left, right)
        for z in range(cz):
            for x in range(cx):
                cell = z * cx + x
                center = source[z, x, rows, :]
                above = source[z, x, above_rows, :]
                beside = (source[z - 1, x, rows, :] if z else halo_z[step, 0, x, rows, :]) + (
                    source[z + 1, x, rows, :] if z < cz - 1 else halo_z[step, 1, x, rows, :])
                beside = beside + (source[z, x - 1, rows, :] if x else halo_x[step, 0, z, rows, :])
                beside = beside + (
                    source[z, x + 1, rows, :] if x < cx - 1 else halo_x[step, 1, z, rows, :])
                face = pltpu.roll(faces, lanes - (2 * cell + 1), 1)
                beside = beside + jnp.where(lane == 0, face, pltpu.roll(center, 1, 1))
                beside = beside + jnp.where(lane == lanes - 1, face, pltpu.roll(center, lanes - 1, 1))
                new = center + diffusion * (beside - 6.0 * center) + losses_above * above
                emit(z, x, new - losses * center)

    def first_step(chunk):
        def emit(z, x, new):
            second[z, x, rows_of[chunk], :] = new
        advance(0, chunk, emit)
        pack_rows(1, chunk)

    def second_step(chunk):
        start = energies - size * (chunk + 1)

        def emit(z, x, new):
            cell = z * cx + x
            out_ref[pl.ds(start * cells + cell, size, stride=cells), :] = new
            shining = gas_ref[cell:cell + 1, :] * new
            high = shining.astype(jnp.bfloat16)
            low = (shining - high.astype(jnp.float32)).astype(jnp.bfloat16)
            lhs[chunk, 0:size, cell * lanes:(cell + 1) * lanes] = high
            lhs[chunk, size:2 * size, cell * lanes:(cell + 1) * lanes] = low
        advance(1, chunk, emit)

    owners = [owner_ref[s] for s in range(slot_count)]
    blocks = [block_ref[s] for s in range(slot_count)]
    ranks = []
    for s in range(slot_count):
        rank = jnp.int32(0)
        for t in range(s):
            rank = rank + jnp.where(owners[t] == owners[s], 1, 0)
        ranks.append(rank)

    chosen = []
    for offset in range(ny):
        who = lax.rem(gy + offset, ny)
        entry = []
        table = jnp.full((8, lanes), -1.0, jnp.float32)
        place = lax.broadcasted_iota(jnp.int32, (8, lanes), 0)
        for c in range(CAP):
            index, name = jnp.int32(0), jnp.int32(-1)
            for s in range(slot_count):
                hit = jnp.logical_and(owners[s] == who, ranks[s] == c)
                index = jnp.where(hit, s, index)
                name = jnp.where(hit, blocks[s], name)
            entry.append(index)
            table = jnp.where(place == c, name.astype(jnp.float32), table)
        chosen.append(entry)
        names[offset] = table

    def sky_copy(chunk, offset):
        return pltpu.make_async_remote_copy(
            src_ref=slots.at[chunk, offset], dst_ref=landed.at[chunk, offset - 1],
            send_sem=sky_send.at[chunk, offset - 1], recv_sem=sky_recv.at[chunk, offset - 1],
            device_id=(gx, lax.rem(gy + offset, ny), gz), device_id_type=MESH,
        )

    def name_copy(offset):
        return pltpu.make_async_remote_copy(
            src_ref=names.at[offset], dst_ref=landed_names.at[offset - 1],
            send_sem=name_send.at[offset - 1], recv_sem=name_recv.at[offset - 1],
            device_id=(gx, lax.rem(gy + offset, ny), gz), device_id_type=MESH,
        )

    def project(chunk):
        for s in range(0, slot_count, 2):
            pair = [weights[t] for t in range(s, min(s + 2, slot_count))]
            rhs = pair[0] if len(pair) == 1 else jnp.concatenate(pair, axis=1)
            product = jnp.dot(lhs[chunk], rhs, preferred_element_type=jnp.float32)
            product = product[0:size] + product[size:2 * size]
            for t in range(len(pair)):
                contrib[chunk, s + t] = product[:, t * lanes:(t + 1) * lanes]
        for offset in range(1, ny):
            for c in range(CAP):
                slots[chunk, offset, c] = contrib[chunk, chosen[offset][c]]
            sky_copy(chunk, offset).start()

    for chunk in range(CHUNKS):
        pack_rows(0, chunk)

    partners = ny - 1
    for side in range(4):
        partners = partners + jnp.where(exists[side], 1, 0)
    pl.semaphore_wait(barrier, partners)

    send_halos(0, 0)
    if CHUNKS > 1:
        send_halos(0, 1)
    for offset in range(1, ny):
        name_copy(offset).start()
    for chunk in range(CHUNKS + 1):
        if chunk < CHUNKS:
            wait_halos(0, chunk)
            first_step(chunk)
            send_halos(1, chunk)
            if chunk + 2 < CHUNKS:
                send_halos(0, chunk + 2)
        if chunk == 1:
            load.wait()
        if chunk:
            wait_halos(1, chunk - 1)
            second_step(chunk - 1)
            project(chunk - 1)

    for offset in range(1, ny):
        name_copy(offset).wait_recv()
    totals = []
    for chunk in range(CHUNKS):
        total = [jnp.zeros((size, lanes), jnp.float32) for _ in range(BO)]
        for offset in range(ny):
            if offset:
                sky_copy(chunk, offset).wait_recv()
            for c in range(CAP):
                if offset:
                    term = landed[chunk, offset - 1, c]
                    name = landed_names[offset - 1, c:c + 1, :]
                else:
                    term = contrib[chunk, chosen[0][c]]
                    name = names[0, c:c + 1, :]
                for b in range(BO):
                    total[b] = total[b] + jnp.where(name == float(b), term, 0.0)
        totals.append(jnp.concatenate(total, axis=1))
    summed = jnp.concatenate(totals[::-1], axis=0)
    sky = jnp.dot(
        pi0_ref[...], summed, precision=lax.Precision.HIGHEST, preferred_element_type=jnp.float32
    )
    for b in range(BO):
        sky_ref[b] = sky[:, b * lanes:(b + 1) * lanes]

    for step in range(2):
        for chunk in range(CHUNKS):
            for side in range(6):
                @pl.when(exists[side])
                def _(step=step, chunk=chunk, side=side):
                    halo_copy(step, chunk, side, False).wait_send()
    for offset in range(1, ny):
        name_copy(offset).wait_send()
        for chunk in range(CHUNKS):
            sky_copy(chunk, offset).wait_send()


def body(sizes, cr_init, gas, diff_coeff, loss_coeff, pi0_table, los_weight, slot_owner, slot_block):
    energies, cz, cx, cy = cr_init.shape
    gammas = pi0_table.shape[0]
    slot_count, cells, pixels = los_weight.shape[3:]
    ny = sizes[1]
    size = energies // CHUNKS
    f32 = jnp.float32
    vmem = pl.BlockSpec(memory_space=pltpu.VMEM)
    smem = pl.BlockSpec(memory_space=pltpu.SMEM)
    density, sky = pl.pallas_call(
        functools.partial(kernel, sizes),
        out_shape=(
            jax.ShapeDtypeStruct((energies * cz * cx, cy), f32),
            jax.ShapeDtypeStruct((BO, gammas, pixels), f32),
        ),
        in_specs=[vmem] * 5 + [smem] * 2 + [pl.BlockSpec(memory_space=pl.ANY)],
        out_specs=(vmem, vmem),
        scratch_shapes=[
            pltpu.VMEM((cz, cx, energies + PAD, cy), f32),
            pltpu.VMEM((cz, cx, energies + PAD, cy), f32),
            pltpu.VMEM((2, 2, cx, energies, cy), f32),
            pltpu.VMEM((2, 2, cz, energies, cy), f32),
            pltpu.VMEM((2, 2, energies, cy), f32),
            pltpu.VMEM((2, energies, cy), f32),
            pltpu.VMEM((3, energies, cy), f32),
            pltpu.VMEM((slot_count, cells, pixels), los_weight.dtype),
            pltpu.VMEM((CHUNKS, 2 * size, cells), jnp.bfloat16),
            pltpu.VMEM((CHUNKS, slot_count, size, pixels), f32),
            pltpu.VMEM((CHUNKS, ny, CAP, size, pixels), f32),
            pltpu.VMEM((CHUNKS, ny - 1, CAP, size, pixels), f32),
            pltpu.VMEM((ny, 8, pixels), f32),
            pltpu.VMEM((ny - 1, 8, pixels), f32),
            pltpu.SemaphoreType.DMA,
            pltpu.SemaphoreType.DMA((2, CHUNKS, 6)),
            pltpu.SemaphoreType.DMA((2, CHUNKS, 6)),
            pltpu.SemaphoreType.DMA((CHUNKS, ny - 1)),
            pltpu.SemaphoreType.DMA((CHUNKS, ny - 1)),
            pltpu.SemaphoreType.DMA((ny - 1,)),
            pltpu.SemaphoreType.DMA((ny - 1,)),
        ],
        compiler_params=pltpu.CompilerParams(
            collective_id=0, has_side_effects=True, vmem_limit_bytes=48 * 1024 * 1024
        ),
    )(
        cr_init.reshape(energies * cz * cx, cy), gas.reshape(cz * cx, cy),
        diff_coeff.reshape(1, energies), loss_coeff.reshape(1, energies), pi0_table,
        slot_owner.reshape(slot_count), slot_block.reshape(slot_count),
        los_weight.reshape(slot_count, cells, pixels),
    )
    return density.reshape(cr_init.shape), sky.reshape(1, 1, BO, gammas, pixels)


def solution(mesh):
    sizes = (mesh.shape["gx"], mesh.shape["gy"], mesh.shape["gz"])
    in_specs = (
        P(None, "gz", "gx", "gy"),
        P("gz", "gx", "gy"),
        P(),
        P(),
        P(),
        P("gz", "gx", "gy", None, None, None),
        P("gz", "gx", "gy", None, None),
        P("gz", "gx", "gy", None),
    )
    out_specs = (P(None, "gz", "gx", "gy"), P("gz", "gx", "gy", None, None))
    return jax.shard_map(
        functools.partial(body, sizes), mesh=mesh, in_specs=in_specs, out_specs=out_specs,
        check_vma=False,
    )
```

time: 133 us -> 36.1 us (0.27)
  waiting for transfers between devices: 51 us -> 0 us
  starting transfers between devices: 31 us -> 0 us
  Pallas kernels: 0 us -> 26.4 us
  other arithmetic: 14.5 us -> 0 us
  between operations: 14.4 us -> 0.66 us
  local copies, waits for them, and re-layouts: 16.6 us -> 8.7 us
  matrix products: 4.73 us -> 0 us
    ppermute x12 -> x0, starting transfers between devices: 31 us -> none  [the longest x6 23.2 us: extended(): lax.ppermute(tail, axis, [(i, (i + 1) % count) for i in range(ends)])]
    reduce_scatter x1 -> x0, waiting for transfers between devices: 27.3 us -> none  [body(): sky = lax.psum_scatter(terms, 'gy', scatter_dimension=0, tiled=True)]
    pallas_call x0 -> x1, Pallas kernels: none -> 26.4 us  [body(): pl.pallas_call(functools.partial(kernel, sizes), out_shape=(jax.ShapeDtyp...]
    ppermute x12 -> x0, waiting for transfers between devices: 23.7 us -> none  [the longest x6 23.5 us: extended(): lax.ppermute(head, axis, [((i + 1) % count, i) for i in range(ends)])]
    slice x8 -> x0, local copies, waits for them, and re-layouts: 7.78 us -> none  [the longest x2 3.25 us: advance(): loss_flux[1:]]
    unnamed x16 -> x17, local copies, waits for them, and re-layouts: 2.66 us -> 8.7 us
    mul x2 -> x0, other arithmetic: 5.71 us -> none  [advance(): loss_flux = losses[:, None, None, None] * center]
    sub x1 -> x0, other arithmetic: 5.43 us -> none  [advance(): center + diffusion[:, None, None, None] * (beside - 6.0 * center)]
  transfers between devices with their start and end apart: 13 -> 0, of which waited for: 9 -> 0; matrix products, arithmetic and copies ran while one was open for 7% -> 0% of each run, Pallas kernels for 0% -> 0%
where the time goes in v1:
time: 36.1 us; the launch traced here: 35.8 us
  Pallas kernels  26.4 us (73%)
  local copies, waits for them, and re-layouts  8.7 us (24%)
  between operations  0.66 us (2%)
    pallas_call x1, Pallas kernels, body(): pl.pallas_call(functools.partial(kernel, sizes), out_shape=(jax.ShapeDtyp...  26.4 us
    unnamed x17, local copies, waits for them, and re-layouts  8.7 us

profile of v1, /device:TPU:0, one launch (start us, length us, event | category | flops | bytes accessed | tf_op | source)
XLA Modules:
  0.0 35.8 jit_solution(12991530114193273509)
XLA Ops:
  0.6 0.8 %copy.10.pi0_ref = f32[96,64]{1,0:T(8,128)S(1)} copy(f32[96,64]{0,1:T(8,128)} %param.12) | data formatting | bytes 49152 | tf_op args[4]
  1.5 0.0 copy-start
  1.5 2.0 %copy-done = bf16[1,1,1,7,2048,128]{5,4,3,2,1,0:T(8,128)(2,1)S(1)} copy-done((bf16[1,1,1,7,2048,128]{5,4,3,2,1,0:T(8,128)(2,1)S(1)}, bf16[1,1,1,7,2048,128]{5,4,3,2,1,0:T(8,128)(2,1)}, u32[]{:S(2)}) %copy-start) | copy-done | bytes 3670040
  3.5 0.0 copy-start.1
  3.5 1.0 %copy-done.1 = f32[64,4,4,128]{3,2,1,0:T(4,128)S(1)} copy-done((f32[64,4,4,128]{3,2,1,0:T(4,128)S(1)}, f32[64,4,4,128]{3,2,1,0:T(4,128)}, u32[]{:S(2)}) %copy-start.1) | copy-done | bytes 524312
  4.6 0.0 copy-start.2
  4.6 0.7 %copy-done.2 = f32[4,4,128]{2,1,0:T(4,128)S(1)} copy-done((f32[4,4,128]{2,1,0:T(4,128)S(1)}, f32[4,4,128]{2,1,0:T(4,128)}, u32[]{:S(2)}) %copy-start.2) | copy-done | bytes 8216
  5.3 0.0 copy-start.3
  5.3 0.7 %copy-done.3 = f32[64]{0:T(128)S(1)} copy-done((f32[64]{0:T(128)S(1)}, f32[64]{0:T(128)}, u32[]{:S(2)}) %copy-start.3) | copy-done | bytes 280
  5.9 0.0 copy-start.4
  5.9 0.7 %copy-done.4 = f32[64]{0:T(128)S(1)} copy-done((f32[64]{0:T(128)S(1)}, f32[64]{0:T(128)}, u32[]{:S(2)}) %copy-start.4) | copy-done | bytes 280
  6.6 0.0 copy-start.5
  6.6 0.7 %copy-done.5 = s32[1,1,1,7,1]{3,4,2,1,0:T(1,128)S(1)} copy-done((s32[1,1,1,7,1]{3,4,2,1,0:T(1,128)S(1)}, s32[1,1,1,7,1]{3,4,2,1,0:T(1,128)}, u32[]{:S(2)}) %copy-start.5) | copy-done | bytes 52
  7.2 0.0 copy-start.6
  7.2 0.7 %copy-done.6 = s32[1,1,1,7]{3,2,1,0:T(1,128)S(1)} copy-done((s32[1,1,1,7]{3,2,1,0:T(1,128)S(1)}, s32[1,1,1,7]{3,2,1,0:T(1,128)}, u32[]{:S(2)}) %copy-start.6) | copy-done | bytes 52
  7.9 26.4 %shard_map.95 = (f32[1024,128]{1,0:T(8,128)S(1)}, f32[4,96,128]{2,1,0:T(8,128)S(1)}) custom-call(f32[1024,128]{1,0:T(8,128)S(1)} %bitcast.11, f32[16,128]{1,0:T(8,128)S(1)} %bitcast.13, f32[1,64]{1,0:T(1,128)S(1)} %bitcast.14, f32[1,64]{1,0:T(1,128)S(1)} %bitcast.15, f32[96,64]{1,0:T(8,128)S(1)} %copy.10.pi0_ref, s32[7]{0:T(128)S(1)} %bitcast.16, ...), custom_call_target="tpu_custom_call" | custom-call | tf_op jit(solution)/shard_map/pallas_call | solution.py:290
  34.3 0.8 %copy.13 = f32[64,4,4,128]{3,2,1,0:T(4,128)} copy(f32[64,4,4,128]{3,2,1,0:T(4,128)S(1)} %bitcast.10) | data formatting | bytes 1048576
  35.1 0.7 %copy.14 = f32[1,1,4,96,128]{4,3,2,1,0:T(8,128)} copy(f32[1,1,4,96,128]{4,3,2,1,0:T(8,128)S(1)} %bitcast.12) | data formatting | bytes 393216
Async XLA Ops:
  1.5 2.0 %copy-start = (bf16[1,1,1,7,2048,128]{5,4,3,2,1,0:T(8,128)(2,1)S(1)}, bf16[1,1,1,7,2048,128]{5,4,3,2,1,0:T(8,128)(2,1)}, u32[]{:S(2)}) copy-start(bf16[1,1,1,7,2048,128]{5,4,3,2,1,0:T(8,128)(2,1)} %param.13) | copy-start | bytes 11010052
  3.5 1.0 %copy-start.1 = (f32[64,4,4,128]{3,2,1,0:T(4,128)S(1)}, f32[64,4,4,128]{3,2,1,0:T(4,128)}, u32[]{:S(2)}) copy-start(f32[64,4,4,128]{3,2,1,0:T(4,128)} %param.8) | copy-start | bytes 1572868
  4.6 0.7 %copy-start.2 = (f32[4,4,128]{2,1,0:T(4,128)S(1)}, f32[4,4,128]{2,1,0:T(4,128)}, u32[]{:S(2)}) copy-start(f32[4,4,128]{2,1,0:T(4,128)} %param.9) | copy-start | bytes 24580
  5.3 0.7 %copy-start.3 = (f32[64]{0:T(128)S(1)}, f32[64]{0:T(128)}, u32[]{:S(2)}) copy-start(f32[64]{0:T(128)} %param.10) | copy-start | bytes 772
  5.9 0.7 %copy-start.4 = (f32[64]{0:T(128)S(1)}, f32[64]{0:T(128)}, u32[]{:S(2)}) copy-start(f32[64]{0:T(128)} %param.11) | copy-start | bytes 772
  6.6 0.7 %copy-start.5 = (s32[1,1,1,7,1]{3,4,2,1,0:T(1,128)S(1)}, s32[1,1,1,7,1]{3,4,2,1,0:T(1,128)}, u32[]{:S(2)}) copy-start(s32[1,1,1,7,1]{3,4,2,1,0:T(1,128)} %param.14) | copy-start | bytes 88
  7.2 0.7 %copy-start.6 = (s32[1,1,1,7]{3,2,1,0:T(1,128)S(1)}, s32[1,1,1,7]{3,2,1,0:T(1,128)}, u32[]{:S(2)}) copy-start(s32[1,1,1,7]{3,2,1,0:T(1,128)} %param.15) | copy-start | bytes 88

commit v2 on v1

--- a/solution.py
+++ b/solution.py
@@ -15,23 +15,21 @@
 
 
 def kernel(
-    sizes, cr_ref, gas_ref, diff_ref, loss_ref, pi0_ref, owner_ref, block_ref, weight_hbm,
-    out_ref, sky_ref,
-    first, second, halo_z, halo_x, halo_y, pack, coef, weights, lhs, contrib, slots, landed,
+    sizes, cr_hbm, gas_hbm, diff_hbm, loss_hbm, pi0_hbm, owner_hbm, block_hbm, weight_hbm,
+    out_hbm, sky_hbm,
+    cr_ref, gas_ref, diff_ref, loss_ref, pi0_ref, owner_ref, block_ref, out_ref, sky_ref,
+    load_sem, out_sem, sky_out_sem, first, second, halo_z, halo_x, halo_y, pack, coef, weights, lhs, contrib, slots, landed,
     names, landed_names,
     weight_sem, halo_send, halo_recv, sky_send, sky_recv, name_send, name_recv,
 ):
     nx, ny, nz = sizes
-    energies = diff_ref.shape[1]
+    energies = diff_hbm.shape[1]
     cz, cx = first.shape[0], first.shape[1]
     lanes = first.shape[3]
     cells = cz * cx
     size = energies // CHUNKS
     slot_count = weights.shape[0]
     gx, gy, gz = lax.axis_index("gx"), lax.axis_index("gy"), lax.axis_index("gz")
-
-    load = pltpu.make_async_copy(weight_hbm, weights, weight_sem)
-    load.start()
 
     exists = (gz > 0, gz < nz - 1, gx > 0, gx < nx - 1, gy > 0, gy < ny - 1)
     places = (
@@ -49,11 +47,26 @@
             barrier, inc=1, device_id=(gx, lax.rem(gy + offset, ny), gz), device_id_type=MESH
         )
 
+    loads = [
+        pltpu.make_async_copy(source, target, load_sem.at[index])
+        for index, (source, target) in enumerate((
+            (cr_hbm, cr_ref), (diff_hbm, diff_ref), (loss_hbm, loss_ref), (gas_hbm, gas_ref),
+            (owner_hbm, owner_ref), (block_hbm, block_ref), (pi0_hbm, pi0_ref),
+        ))
+    ]
+    for copy in loads:
+        copy.start()
+    load = pltpu.make_async_copy(weight_hbm, weights, weight_sem)
+    load.start()
+
+    loads[0].wait()
     for cell in range(cells):
         first[cell // cx, cell % cx, 0:energies, :] = cr_ref[pl.ds(cell, energies, stride=cells), :]
     first[:, :, energies:, :] = jnp.zeros((cz, cx, PAD, lanes), jnp.float32)
     second[:, :, energies:, :] = jnp.zeros((cz, cx, PAD, lanes), jnp.float32)
 
+    for copy in loads[1:]:
+        copy.wait()
     row = lax.broadcasted_iota(jnp.int32, (energies, energies), 0)
     column = lax.broadcasted_iota(jnp.int32, (energies, energies), 1)
     diff = jnp.broadcast_to(diff_ref[...], (energies, energies))
@@ -160,6 +173,11 @@
             lhs[chunk, 0:size, cell * lanes:(cell + 1) * lanes] = high
             lhs[chunk, size:2 * size, cell * lanes:(cell + 1) * lanes] = low
         advance(1, chunk, emit)
+        out_copy(chunk).start()
+
+    def out_copy(chunk):
+        part = pl.ds((energies - size * (chunk + 1)) * cells, size * cells)
+        return pltpu.make_async_copy(out_ref.at[part, :], out_hbm.at[part, :], out_sem.at[chunk])
 
     owners = [owner_ref[s] for s in range(slot_count)]
     blocks = [block_ref[s] for s in range(slot_count)]
@@ -261,10 +279,12 @@
         totals.append(jnp.concatenate(total, axis=1))
     summed = jnp.concatenate(totals[::-1], axis=0)
     sky = jnp.dot(
-        pi0_ref[...], summed, precision=lax.Precision.HIGHEST, preferred_element_type=jnp.float32
+        pi0_ref[...].T, summed, precision=lax.Precision.HIGHEST, preferred_element_type=jnp.float32
     )
     for b in range(BO):
         sky_ref[b] = sky[:, b * lanes:(b + 1) * lanes]
+    sky_out = pltpu.make_async_copy(sky_ref, sky_hbm, sky_out_sem)
+    sky_out.start()
 
     for step in range(2):
         for chunk in range(CHUNKS):
@@ -276,6 +296,9 @@
         name_copy(offset).wait_send()
         for chunk in range(CHUNKS):
             sky_copy(chunk, offset).wait_send()
+    for chunk in range(CHUNKS):
+        out_copy(chunk).wait()
+    sky_out.wait()
 
 
 def body(sizes, cr_init, gas, diff_coeff, loss_coeff, pi0_table, los_weight, slot_owner, slot_block):
@@ -285,17 +308,28 @@
     ny = sizes[1]
     size = energies // CHUNKS
     f32 = jnp.float32
-    vmem = pl.BlockSpec(memory_space=pltpu.VMEM)
-    smem = pl.BlockSpec(memory_space=pltpu.SMEM)
+    anywhere = pl.BlockSpec(memory_space=pl.ANY)
     density, sky = pl.pallas_call(
         functools.partial(kernel, sizes),
         out_shape=(
             jax.ShapeDtypeStruct((energies * cz * cx, cy), f32),
             jax.ShapeDtypeStruct((BO, gammas, pixels), f32),
         ),
-        in_specs=[vmem] * 5 + [smem] * 2 + [pl.BlockSpec(memory_space=pl.ANY)],
-        out_specs=(vmem, vmem),
+        in_specs=[anywhere] * 8,
+        out_specs=(anywhere, anywhere),
         scratch_shapes=[
+            pltpu.VMEM((energies * cz * cx, cy), f32),
+            pltpu.VMEM((cz * cx, cy), f32),
+            pltpu.VMEM((1, energies), f32),
+            pltpu.VMEM((1, energies), f32),
+            pltpu.VMEM((energies, gammas), f32),
+            pltpu.SMEM((slot_count,), jnp.int32),
+            pltpu.SMEM((slot_count,), jnp.int32),
+            pltpu.VMEM((energies * cz * cx, cy), f32),
+            pltpu.VMEM((BO, gammas, pixels), f32),
+            pltpu.SemaphoreType.DMA((7,)),
+            pltpu.SemaphoreType.DMA((CHUNKS,)),
+            pltpu.SemaphoreType.DMA,
             pltpu.VMEM((cz, cx, energies + PAD, cy), f32),
             pltpu.VMEM((cz, cx, energies + PAD, cy), f32),
             pltpu.VMEM((2, 2, cx, energies, cy), f32),
@@ -319,11 +353,11 @@
             pltpu.SemaphoreType.DMA((ny - 1,)),
         ],
         compiler_params=pltpu.CompilerParams(
-            collective_id=0, has_side_effects=True, vmem_limit_bytes=48 * 1024 * 1024
+            collective_id=0, has_side_effects=True, vmem_limit_bytes=63 * 1024 * 1024
         ),
     )(
         cr_init.reshape(energies * cz * cx, cy), gas.reshape(cz * cx, cy),
-        diff_coeff.reshape(1, energies), loss_coeff.reshape(1, energies), pi0_table,
+        diff_coeff.reshape(1, energies), loss_coeff.reshape(1, energies), pi0_table.T,
         slot_owner.reshape(slot_count), slot_block.reshape(slot_count),
         los_weight.reshape(slot_count, cells, pixels),
     )

time: 36.1 us -> 31.3 us (0.87)
  local copies, waits for them, and re-layouts: 8.7 us -> 3.48 us
  Pallas kernels: 26.4 us -> 27 us
    unnamed x17 -> x2, local copies, waits for them, and re-layouts: 8.7 us -> 3.48 us
    pallas_call x1, Pallas kernels: 26.4 us -> 27 us  [body(): pl.pallas_call(functools.partial(kernel, sizes), out_shape=(jax.ShapeDtyp...]
where the time goes in v2:
time: 31.3 us; the launch traced here: 31.1 us
  Pallas kernels  27 us (86%)
  local copies, waits for them, and re-layouts  3.48 us (11%)
  between operations  0.64 us (2%)
    pallas_call x1, Pallas kernels, body(): pl.pallas_call(functools.partial(kernel, sizes), out_shape=(jax.ShapeDtyp...  27 us
    unnamed x2, local copies, waits for them, and re-layouts  3.48 us

profile of v2, /device:TPU:0, one launch (start us, length us, event | category | flops | bytes accessed | tf_op | source)
XLA Modules:
  0.0 31.1 jit_solution(14431412625681711455)
XLA Ops:
  0.6 27.0 %shard_map.95 = (f32[1024,128]{1,0:T(8,128)}, f32[4,96,128]{2,1,0:T(8,128)}) custom-call(f32[1024,128]{1,0:T(8,128)} %bitcast.12, f32[16,128]{1,0:T(8,128)} %bitcast.15, f32[1,64]{1,0:T(1,128)} %bitcast.16, f32[1,64]{1,0:T(1,128)} %bitcast.17, f32[64,96]{1,0:T(8,128)} %bitcast.14, s32[7]{0:T(128)} %bitcast.18, s32[7]{0:T(128)} %bitcast.19, ...), custom_call_target="tpu_custom_call" | custom-call | tf_op jit(solution)/shard_map/pallas_call | solution.py:312
  27.6 1.9 %copy.12 = f32[64,4,4,128]{3,2,1,0:T(4,128)} copy(f32[64,4,4,128]{3,2,1,0:T(4,128)} %bitcast.11) | data formatting | bytes 1048576
  29.5 1.6 %copy.13 = f32[1,1,4,96,128]{4,3,2,1,0:T(8,128)} copy(f32[1,1,4,96,128]{4,3,2,1,0:T(8,128)} %bitcast.13) | data formatting | bytes 393216

commit v3 on v2

--- a/solution.py
+++ b/solution.py
@@ -20,6 +20,7 @@
     cr_ref, gas_ref, diff_ref, loss_ref, pi0_ref, owner_ref, block_ref, out_ref, sky_ref,
     load_sem, out_sem, sky_out_sem, first, second, halo_z, halo_x, halo_y, pack, coef, weights, lhs, contrib, slots, landed,
     names, landed_names,
+    relay, relay_in_send, relay_in_recv, relay_out_send, half_recv,
     weight_sem, halo_send, halo_recv, sky_send, sky_recv, name_send, name_recv,
 ):
     nx, ny, nz = sizes
@@ -31,7 +32,14 @@
     slot_count = weights.shape[0]
     gx, gy, gz = lax.axis_index("gx"), lax.axis_index("gy"), lax.axis_index("gz")
 
+    bent = nx == 2 and nz == 4
+    middle = jnp.logical_and(gz > 0, gz < nz - 1)
+    real = (gz > 0, gz < nz - 1, gx > 0, gx < nx - 1, gy > 0, gy < ny - 1)
     exists = (gz > 0, gz < nz - 1, gx > 0, gx < nx - 1, gy > 0, gy < ny - 1)
+    if bent:
+        exists = (
+            jnp.logical_and(gz > 0, gz != 2), jnp.logical_and(gz < nz - 1, gz != 1),
+        ) + exists[2:]
     places = (
         (gx, gy, gz - 1), (gx, gy, gz + 1), (gx - 1, gy, gz), (gx + 1, gy, gz),
         (gx, gy - 1, gz), (gx, gy + 1, gz),
@@ -42,6 +50,10 @@
         @pl.when(exists[side])
         def _(side=side):
             pl.semaphore_signal(barrier, inc=1, device_id=places[side], device_id_type=MESH)
+    if bent:
+        pl.semaphore_signal(
+            barrier, inc=1, device_id=(gx, gy, lax.rem(gz + 2, nz)), device_id_type=MESH
+        )
     for offset in range(1, ny):
         pl.semaphore_signal(
             barrier, inc=1, device_id=(gx, lax.rem(gy + offset, ny), gz), device_id_type=MESH
@@ -78,7 +90,7 @@
         coef[index] = jnp.broadcast_to(spread, (energies, lanes))
 
     for side in range(6):
-        @pl.when(jnp.logical_not(exists[side]))
+        @pl.when(jnp.logical_not(real[side]))
         def _(side=side):
             halo = (halo_z, halo_x, halo_y)[side // 2]
             for step in range(2):
@@ -111,6 +123,41 @@
             device_id=places[side], device_id_type=MESH,
         )
 
+    half = cx // 2
+    way = lax.rem(gz + 1, 2)
+
+    def relay_in(step, chunk, part):
+        face = (first, second)[step].at[(cz - 1) * (1 - way)]
+        return pltpu.make_async_remote_copy(
+            src_ref=face.at[pl.ds(part * half, half), rows_of[chunk], :],
+            dst_ref=relay.at[step, way, :, rows_of[chunk], :],
+            send_sem=relay_in_send.at[step, chunk, part],
+            recv_sem=relay_in_recv.at[step, chunk, way],
+            device_id=(gx, gy, part * (nz - 1)), device_id_type=MESH,
+        )
+
+    def relay_out(step, chunk, going):
+        part = lax.rem(gz, 2)
+        return pltpu.make_async_remote_copy(
+            src_ref=relay.at[step, going, :, rows_of[chunk], :],
+            dst_ref=halo_z.at[step, going, pl.ds(part * half, half), rows_of[chunk], :],
+            send_sem=relay_out_send.at[step, chunk, going],
+            recv_sem=half_recv.at[step, chunk, part],
+            device_id=(gx, gy, 2 - going), device_id_type=MESH,
+        )
+
+    def relay_wait(step, chunk, part, going):
+        if going is not None:
+            place = relay.at[step, going, :, rows_of[chunk], :]
+            sem = relay_in_recv.at[step, chunk, going]
+        else:
+            place = halo_z.at[step, 1 - way, pl.ds(part * half, half), rows_of[chunk], :]
+            sem = half_recv.at[step, chunk, part]
+        return pltpu.make_async_remote_copy(
+            src_ref=place, dst_ref=place, send_sem=relay_in_send.at[step, chunk, 0], recv_sem=sem,
+            device_id=(gx, gy, lax.rem(gz + 2, nz)), device_id_type=MESH,
+        )
+
     def pack_rows(step, chunk):
         source = (first, second)[step]
         packed = jnp.zeros((size, lanes), jnp.float32)
@@ -120,12 +167,28 @@
         pack[step, rows_of[chunk], :] = packed
 
     def send_halos(step, chunk):
+        if bent:
+            @pl.when(middle)
+            def _():
+                for part in range(2):
+                    relay_in(step, chunk, part).start()
         for side in range(6):
             @pl.when(exists[side])
             def _(side=side):
                 halo_copy(step, chunk, side, False).start()
 
     def wait_halos(step, chunk):
+        if bent:
+            @pl.when(jnp.logical_not(middle))
+            def _():
+                for going in range(2):
+                    relay_wait(step, chunk, 0, going).wait_recv()
+                    relay_out(step, chunk, going).start()
+
+            @pl.when(middle)
+            def _():
+                for part in range(2):
+                    relay_wait(step, chunk, part, None).wait_recv()
         for side in range(6):
             @pl.when(exists[side])
             def _(side=side):
@@ -235,7 +298,7 @@
     for chunk in range(CHUNKS):
         pack_rows(0, chunk)
 
-    partners = ny - 1
+    partners = ny - 1 + (1 if bent else 0)
     for side in range(4):
         partners = partners + jnp.where(exists[side], 1, 0)
     pl.semaphore_wait(barrier, partners)
@@ -288,6 +351,16 @@
 
     for step in range(2):
         for chunk in range(CHUNKS):
+            if bent:
+                @pl.when(middle)
+                def _(step=step, chunk=chunk):
+                    for part in range(2):
+                        relay_in(step, chunk, part).wait_send()
+
+                @pl.when(jnp.logical_not(middle))
+                def _(step=step, chunk=chunk):
+                    for going in range(2):
+                        relay_out(step, chunk, going).wait_send()
             for side in range(6):
                 @pl.when(exists[side])
                 def _(step=step, chunk=chunk, side=side):
@@ -299,6 +372,22 @@
     for chunk in range(CHUNKS):
         out_copy(chunk).wait()
     sky_out.wait()
+
+
+def hand_over(density_in, sky_in, density_out, sky_out, sems):
+    rows = density_in.shape[0] // 4
+    copies = [
+        pltpu.make_async_copy(
+            density_in.at[pl.ds(i * rows, rows), :], density_out.at[pl.ds(i * rows, rows), :],
+            sems.at[i],
+        )
+        for i in range(4)
+    ]
+    copies.append(pltpu.make_async_copy(sky_in, sky_out, sems.at[4]))
+    for copy in copies:
+        copy.start()
+    for copy in copies:
+        copy.wait()
 
 
 def body(sizes, cr_init, gas, diff_coeff, loss_coeff, pi0_table, los_weight, slot_owner, slot_block):
@@ -344,6 +433,11 @@
             pltpu.VMEM((CHUNKS, ny - 1, CAP, size, pixels), f32),
             pltpu.VMEM((ny, 8, pixels), f32),
             pltpu.VMEM((ny - 1, 8, pixels), f32),
+            pltpu.VMEM((2, 2, cx // 2, energies, cy), f32),
+            pltpu.SemaphoreType.DMA((2, CHUNKS, 2)),
+            pltpu.SemaphoreType.DMA((2, CHUNKS, 2)),
+            pltpu.SemaphoreType.DMA((2, CHUNKS, 2)),
+            pltpu.SemaphoreType.DMA((2, CHUNKS, 2)),
             pltpu.SemaphoreType.DMA,
             pltpu.SemaphoreType.DMA((2, CHUNKS, 6)),
             pltpu.SemaphoreType.DMA((2, CHUNKS, 6)),
@@ -361,6 +455,16 @@
         slot_owner.reshape(slot_count), slot_block.reshape(slot_count),
         los_weight.reshape(slot_count, cells, pixels),
     )
+    density, sky = pl.pallas_call(
+        hand_over,
+        out_shape=(
+            jax.ShapeDtypeStruct(density.shape, f32), jax.ShapeDtypeStruct(sky.shape, f32),
+        ),
+        in_specs=[anywhere] * 2,
+        out_specs=(anywhere, anywhere),
+        scratch_shapes=[pltpu.SemaphoreType.DMA((5,))],
+        compiler_params=pltpu.CompilerParams(vmem_limit_bytes=63 * 1024 * 1024),
+    )(density, sky)
     return density.reshape(cr_init.shape), sky.reshape(1, 1, BO, gammas, pixels)
 
 

time: 31.3 us -> 54.7 us (1.75)
  Pallas kernels: 27 us -> 53.5 us
  local copies, waits for them, and re-layouts: 3.48 us -> 0 us
    pallas_call x0 -> x1, Pallas kernels: none -> 23 us  [body(): pl.pallas_call(hand_over, out_shape=(jax.ShapeDtypeStruct(density.shape,...]
    pallas_call x1, Pallas kernels: 27 us -> 30.5 us  [body(): pl.pallas_call(functools.partial(kernel, sizes), out_shape=(jax.ShapeDtyp...]
    unnamed x2 -> x0, local copies, waits for them, and re-layouts: 3.48 us -> none
where the time goes in v3:
time: 54.7 us; the launch traced here: 54.1 us
  Pallas kernels  53.5 us (98%)
  between operations  0.64 us (1%)
    pallas_call x1, Pallas kernels, body(): pl.pallas_call(functools.partial(kernel, sizes), out_shape=(jax.ShapeDtyp...  30.5 us
    pallas_call x1, Pallas kernels, body(): pl.pallas_call(hand_over, out_shape=(jax.ShapeDtypeStruct(density.shape,...  23 us

profile of v3, /device:TPU:0, one launch (start us, length us, event | category | flops | bytes accessed | tf_op | source)
XLA Modules:
  0.0 54.1 jit_solution(9782508469392094994)
XLA Ops:
  0.6 30.5 %shard_map.95 = (f32[1024,128]{1,0:T(8,128)}, f32[4,96,128]{2,1,0:T(8,128)}) custom-call(f32[1024,128]{1,0:T(8,128)} %bitcast.11, f32[16,128]{1,0:T(8,128)} %bitcast.13, f32[1,64]{1,0:T(1,128)} %bitcast.14, f32[1,64]{1,0:T(1,128)} %bitcast.15, f32[64,96]{1,0:T(8,128)} %bitcast.12, s32[7]{0:T(128)} %bitcast.16, s32[7]{0:T(128)} %bitcast.17, ...), custom_call_target="tpu_custom_call" | custom-call | tf_op jit(solution)/shard_map/pallas_call | solution.py:401
  31.2 23.0 %shard_map.96 = (f32[1024,128]{1,0:T(8,128)}, f32[4,96,128]{2,1,0:T(8,128)}) custom-call(f32[1024,128]{1,0:T(8,128)} %get-tuple-element.6.density_in, f32[4,96,128]{2,1,0:T(8,128)} %get-tuple-element.7.sky_in), custom_call_target="tpu_custom_call" | custom-call | tf_op jit(solution)/shard_map/pallas_call | solution.py:458

commit v4 on v2

--- a/solution.py
+++ b/solution.py
@@ -9,7 +9,7 @@
 
 BO = 4
 CAP = 3
-CHUNKS = 4
+CHUNKS = 2
 PAD = 8
 MESH = pl.DeviceIdType.MESH
 
@@ -299,6 +299,27 @@
     for chunk in range(CHUNKS):
         out_copy(chunk).wait()
     sky_out.wait()
+
+
+def hand_over(density_in, sky_in, density_out, sky_out, density, sky, sems):
+    parts = sems.shape[1] - 1
+    rows = density_in.shape[0] // parts
+    bounds = [pl.ds(i * rows, rows) for i in range(parts)]
+    arriving = [
+        pltpu.make_async_copy(density_in.at[part, :], density.at[part, :], sems.at[0, i])
+        for i, part in enumerate(bounds)
+    ] + [pltpu.make_async_copy(sky_in, sky, sems.at[0, parts])]
+    leaving = [
+        pltpu.make_async_copy(density.at[part, :], density_out.at[part, :], sems.at[1, i])
+        for i, part in enumerate(bounds)
+    ] + [pltpu.make_async_copy(sky, sky_out, sems.at[1, parts])]
+    for copy in arriving:
+        copy.start()
+    for copy, onward in zip(arriving, leaving):
+        copy.wait()
+        onward.start()
+    for copy in leaving:
+        copy.wait()
 
 
 def body(sizes, cr_init, gas, diff_coeff, loss_coeff, pi0_table, los_weight, slot_owner, slot_block):
@@ -361,6 +382,20 @@
         slot_owner.reshape(slot_count), slot_block.reshape(slot_count),
         los_weight.reshape(slot_count, cells, pixels),
     )
+    density, sky = pl.pallas_call(
+        hand_over,
+        out_shape=(
+            jax.ShapeDtypeStruct(density.shape, f32), jax.ShapeDtypeStruct(sky.shape, f32),
+        ),
+        in_specs=[anywhere] * 2,
+        out_specs=(anywhere, anywhere),
+        scratch_shapes=[
+            pltpu.VMEM(density.shape, f32),
+            pltpu.VMEM(sky.shape, f32),
+            pltpu.SemaphoreType.DMA((2, 5)),
+        ],
+        compiler_params=pltpu.CompilerParams(vmem_limit_bytes=63 * 1024 * 1024),
+    )(density, sky)
     return density.reshape(cr_init.shape), sky.reshape(1, 1, BO, gammas, pixels)
 
 

time: 31.3 us -> 28.6 us (0.914)
  local copies, waits for them, and re-layouts: 3.48 us -> 0 us
  Pallas kernels: 27 us -> 27.8 us
    unnamed x2 -> x0, local copies, waits for them, and re-layouts: 3.48 us -> none
    pallas_call x0 -> x1, Pallas kernels: none -> 1.95 us  [body(): pl.pallas_call(hand_over, out_shape=(jax.ShapeDtypeStruct(density.shape,...]
    pallas_call x1, Pallas kernels: 27 us -> 25.9 us  [body(): pl.pallas_call(functools.partial(kernel, sizes), out_shape=(jax.ShapeDtyp...]
where the time goes in v4:
time: 28.6 us; the launch traced here: 28.4 us
  Pallas kernels  27.8 us (97%)
  between operations  0.64 us (2%)
    pallas_call x1, Pallas kernels, body(): pl.pallas_call(functools.partial(kernel, sizes), out_shape=(jax.ShapeDtyp...  25.9 us
    pallas_call x1, Pallas kernels, body(): pl.pallas_call(hand_over, out_shape=(jax.ShapeDtypeStruct(density.shape,...  1.95 us

profile of v4, /device:TPU:0, one launch (start us, length us, event | category | flops | bytes accessed | tf_op | source)
XLA Modules:
  0.0 28.4 jit_solution(11502491978435488159)
XLA Ops:
  0.6 25.9 %shard_map.95 = (f32[1024,128]{1,0:T(8,128)}, f32[4,96,128]{2,1,0:T(8,128)}) custom-call(f32[1024,128]{1,0:T(8,128)} %bitcast.11, f32[16,128]{1,0:T(8,128)} %bitcast.13, f32[1,64]{1,0:T(1,128)} %bitcast.14, f32[1,64]{1,0:T(1,128)} %bitcast.15, f32[64,96]{1,0:T(8,128)} %bitcast.12, s32[7]{0:T(128)} %bitcast.16, s32[7]{0:T(128)} %bitcast.17, ...), custom_call_target="tpu_custom_call" | custom-call | tf_op jit(solution)/shard_map/pallas_call | solution.py:333
  26.5 2.0 %shard_map.96 = (f32[1024,128]{1,0:T(8,128)}, f32[4,96,128]{2,1,0:T(8,128)}) custom-call(f32[1024,128]{1,0:T(8,128)} %get-tuple-element.6.density_in, f32[4,96,128]{2,1,0:T(8,128)} %get-tuple-element.7.sky_in), custom_call_target="tpu_custom_call" | custom-call | tf_op jit(solution)/shard_map/pallas_call | solution.py:385

commit v5 on v4

--- a/solution.py
+++ b/solution.py
@@ -62,27 +62,6 @@
     loads[0].wait()
     for cell in range(cells):
         first[cell // cx, cell % cx, 0:energies, :] = cr_ref[pl.ds(cell, energies, stride=cells), :]
-    first[:, :, energies:, :] = jnp.zeros((cz, cx, PAD, lanes), jnp.float32)
-    second[:, :, energies:, :] = jnp.zeros((cz, cx, PAD, lanes), jnp.float32)
-
-    for copy in loads[1:]:
-        copy.wait()
-    row = lax.broadcasted_iota(jnp.int32, (energies, energies), 0)
-    column = lax.broadcasted_iota(jnp.int32, (energies, energies), 1)
-    diff = jnp.broadcast_to(diff_ref[...], (energies, energies))
-    loss = jnp.broadcast_to(loss_ref[...], (energies, energies))
-    for index, (values, mask) in enumerate(
-        ((diff, row == column), (loss, row == column), (loss, row + 1 == column))
-    ):
-        spread = jnp.sum(jnp.where(mask, values, 0.0), axis=1, keepdims=True)
-        coef[index] = jnp.broadcast_to(spread, (energies, lanes))
-
-    for side in range(6):
-        @pl.when(jnp.logical_not(exists[side]))
-        def _(side=side):
-            halo = (halo_z, halo_x, halo_y)[side // 2]
-            for step in range(2):
-                halo[step, side % 2] = jnp.zeros(halo.shape[2:], jnp.float32)
 
     lane = lax.broadcasted_iota(jnp.int32, (size, lanes), 1)
     rows_of = [pl.ds(energies - size * (c + 1), size) for c in range(CHUNKS)]
@@ -119,8 +98,8 @@
             packed = jnp.where(lane // 2 == cell, turned, packed)
         pack[step, rows_of[chunk], :] = packed
 
-    def send_halos(step, chunk):
-        for side in range(6):
+    def send_halos(step, chunk, sides):
+        for side in sides:
             @pl.when(exists[side])
             def _(side=side):
                 halo_copy(step, chunk, side, False).start()
@@ -131,7 +110,7 @@
             def _(side=side):
                 halo_copy(step, chunk, side, True).wait_recv()
 
-    def advance(step, chunk, emit):
+    def advance(step, chunk, emit, planes):
         source = (first, second)[step]
         rows = rows_of[chunk]
         above_rows = pl.ds(energies - size * (chunk + 1) + 1, size)
@@ -139,7 +118,7 @@
         left = pltpu.roll(halo_y[step, 0, rows, :], 1, 1)
         right = pltpu.roll(halo_y[step, 1, rows, :], lanes - 1, 1)
         faces = jnp.where(lane % 2 == 1, left, right)
-        for z in range(cz):
+        for z in planes:
             for x in range(cx):
                 cell = z * cx + x
                 center = source[z, x, rows, :]
@@ -158,8 +137,12 @@
     def first_step(chunk):
         def emit(z, x, new):
             second[z, x, rows_of[chunk], :] = new
-        advance(0, chunk, emit)
+        advance(0, chunk, emit, sorted({0, cz - 1}))
+        send_halos(1, chunk, range(2))
+        advance(0, chunk, emit, range(1, cz - 1))
+        send_halos(1, chunk, range(2, 4))
         pack_rows(1, chunk)
+        send_halos(1, chunk, range(4, 6))
 
     def second_step(chunk):
         start = energies - size * (chunk + 1)
@@ -172,12 +155,72 @@
             low = (shining - high.astype(jnp.float32)).astype(jnp.bfloat16)
             lhs[chunk, 0:size, cell * lanes:(cell + 1) * lanes] = high
             lhs[chunk, size:2 * size, cell * lanes:(cell + 1) * lanes] = low
-        advance(1, chunk, emit)
+        advance(1, chunk, emit, range(cz))
         out_copy(chunk).start()
 
     def out_copy(chunk):
         part = pl.ds((energies - size * (chunk + 1)) * cells, size * cells)
         return pltpu.make_async_copy(out_ref.at[part, :], out_hbm.at[part, :], out_sem.at[chunk])
+
+    def sky_copy(chunk, offset):
+        return pltpu.make_async_remote_copy(
+            src_ref=slots.at[chunk, offset], dst_ref=landed.at[chunk, offset - 1],
+            send_sem=sky_send.at[chunk, offset - 1], recv_sem=sky_recv.at[chunk, offset - 1],
+            device_id=(gx, lax.rem(gy + offset, ny), gz), device_id_type=MESH,
+        )
+
+    def name_copy(offset):
+        return pltpu.make_async_remote_copy(
+            src_ref=names.at[offset], dst_ref=landed_names.at[offset - 1],
+            send_sem=name_send.at[offset - 1], recv_sem=name_recv.at[offset - 1],
+            device_id=(gx, lax.rem(gy + offset, ny), gz), device_id_type=MESH,
+        )
+
+    def project(chunk):
+        for s in range(0, slot_count, 2):
+            pair = [weights[t] for t in range(s, min(s + 2, slot_count))]
+            rhs = pair[0] if len(pair) == 1 else jnp.concatenate(pair, axis=1)
+            product = jnp.dot(lhs[chunk], rhs, preferred_element_type=jnp.float32)
+            product = product[0:size] + product[size:2 * size]
+            for t in range(len(pair)):
+                contrib[chunk, s + t] = product[:, t * lanes:(t + 1) * lanes]
+        for offset in range(1, ny):
+            for c in range(CAP):
+                slots[chunk, offset, c] = contrib[chunk, chosen[offset][c]]
+            sky_copy(chunk, offset).start()
+
+    partners = ny - 1
+    for side in range(4):
+        partners = partners + jnp.where(exists[side], 1, 0)
+    pl.semaphore_wait(barrier, partners)
+
+    for chunk in range(min(2, CHUNKS)):
+        send_halos(0, chunk, range(4))
+    for chunk in range(CHUNKS):
+        pack_rows(0, chunk)
+        if chunk < 2:
+            send_halos(0, chunk, range(4, 6))
+
+    for copy in loads[1:]:
+        copy.wait()
+    row = lax.broadcasted_iota(jnp.int32, (energies, energies), 0)
+    column = lax.broadcasted_iota(jnp.int32, (energies, energies), 1)
+    diff = jnp.broadcast_to(diff_ref[...], (energies, energies))
+    loss = jnp.broadcast_to(loss_ref[...], (energies, energies))
+    for index, (values, mask) in enumerate(
+        ((diff, row == column), (loss, row == column), (loss, row + 1 == column))
+    ):
+        spread = jnp.sum(jnp.where(mask, values, 0.0), axis=1, keepdims=True)
+        coef[index] = jnp.broadcast_to(spread, (energies, lanes))
+
+    for side in range(6):
+        @pl.when(jnp.logical_not(exists[side]))
+        def _(side=side):
+            halo = (halo_z, halo_x, halo_y)[side // 2]
+            for step in range(2):
+                halo[step, side % 2] = jnp.zeros(halo.shape[2:], jnp.float32)
+    first[:, :, energies:, :] = jnp.zeros((cz, cx, PAD, lanes), jnp.float32)
+    second[:, :, energies:, :] = jnp.zeros((cz, cx, PAD, lanes), jnp.float32)
 
     owners = [owner_ref[s] for s in range(slot_count)]
     blocks = [block_ref[s] for s in range(slot_count)]
@@ -205,53 +248,14 @@
         chosen.append(entry)
         names[offset] = table
 
-    def sky_copy(chunk, offset):
-        return pltpu.make_async_remote_copy(
-            src_ref=slots.at[chunk, offset], dst_ref=landed.at[chunk, offset - 1],
-            send_sem=sky_send.at[chunk, offset - 1], recv_sem=sky_recv.at[chunk, offset - 1],
-            device_id=(gx, lax.rem(gy + offset, ny), gz), device_id_type=MESH,
-        )
-
-    def name_copy(offset):
-        return pltpu.make_async_remote_copy(
-            src_ref=names.at[offset], dst_ref=landed_names.at[offset - 1],
-            send_sem=name_send.at[offset - 1], recv_sem=name_recv.at[offset - 1],
-            device_id=(gx, lax.rem(gy + offset, ny), gz), device_id_type=MESH,
-        )
-
-    def project(chunk):
-        for s in range(0, slot_count, 2):
-            pair = [weights[t] for t in range(s, min(s + 2, slot_count))]
-            rhs = pair[0] if len(pair) == 1 else jnp.concatenate(pair, axis=1)
-            product = jnp.dot(lhs[chunk], rhs, preferred_element_type=jnp.float32)
-            product = product[0:size] + product[size:2 * size]
-            for t in range(len(pair)):
-                contrib[chunk, s + t] = product[:, t * lanes:(t + 1) * lanes]
-        for offset in range(1, ny):
-            for c in range(CAP):
-                slots[chunk, offset, c] = contrib[chunk, chosen[offset][c]]
-            sky_copy(chunk, offset).start()
-
-    for chunk in range(CHUNKS):
-        pack_rows(0, chunk)
-
-    partners = ny - 1
-    for side in range(4):
-        partners = partners + jnp.where(exists[side], 1, 0)
-    pl.semaphore_wait(barrier, partners)
-
-    send_halos(0, 0)
-    if CHUNKS > 1:
-        send_halos(0, 1)
     for offset in range(1, ny):
         name_copy(offset).start()
     for chunk in range(CHUNKS + 1):
         if chunk < CHUNKS:
             wait_halos(0, chunk)
             first_step(chunk)
-            send_halos(1, chunk)
             if chunk + 2 < CHUNKS:
-                send_halos(0, chunk + 2)
+                send_halos(0, chunk + 2, range(6))
         if chunk == 1:
             load.wait()
         if chunk:

time: 28.6 us -> 28.2 us (0.986)
  Pallas kernels: 27.8 us -> 27.4 us
    pallas_call x1, Pallas kernels: 25.9 us -> 25.4 us  [body(): pl.pallas_call(functools.partial(kernel, sizes), out_shape=(jax.ShapeDtyp...]
where the time goes in v5:
time: 28.2 us; the launch traced here: 28 us
  Pallas kernels  27.4 us (97%)
  between operations  0.64 us (2%)
    pallas_call x1, Pallas kernels, body(): pl.pallas_call(functools.partial(kernel, sizes), out_shape=(jax.ShapeDtyp...  25.4 us
    pallas_call x1, Pallas kernels, body(): pl.pallas_call(hand_over, out_shape=(jax.ShapeDtypeStruct(density.shape,...  1.95 us

profile of v5, /device:TPU:0, one launch (start us, length us, event | category | flops | bytes accessed | tf_op | source)
XLA Modules:
  0.0 28.0 jit_solution(416268624839659688)
XLA Ops:
  0.6 25.4 %shard_map.95 = (f32[1024,128]{1,0:T(8,128)}, f32[4,96,128]{2,1,0:T(8,128)}) custom-call(f32[1024,128]{1,0:T(8,128)} %bitcast.11, f32[16,128]{1,0:T(8,128)} %bitcast.13, f32[1,64]{1,0:T(1,128)} %bitcast.14, f32[1,64]{1,0:T(1,128)} %bitcast.15, f32[64,96]{1,0:T(8,128)} %bitcast.12, s32[7]{0:T(128)} %bitcast.16, s32[7]{0:T(128)} %bitcast.17, ...), custom_call_target="tpu_custom_call" | custom-call | tf_op jit(solution)/shard_map/pallas_call | solution.py:337
  26.1 2.0 %shard_map.96 = (f32[1024,128]{1,0:T(8,128)}, f32[4,96,128]{2,1,0:T(8,128)}) custom-call(f32[1024,128]{1,0:T(8,128)} %get-tuple-element.6.density_in, f32[4,96,128]{2,1,0:T(8,128)} %get-tuple-element.7.sky_in), custom_call_target="tpu_custom_call" | custom-call | tf_op jit(solution)/shard_map/pallas_call | solution.py:389

commit v6 on v5

--- a/solution.py
+++ b/solution.py
@@ -9,7 +9,7 @@
 
 BO = 4
 CAP = 3
-CHUNKS = 2
+CHUNKS = 1
 PAD = 8
 MESH = pl.DeviceIdType.MESH
 

time: 28.2 us -> 29.1 us (1.032)
  the two profiles are of different devices: /device:TPU:0 before, /device:TPU:12 now
where the time goes in v6:
time: 29.1 us; the launch traced here: 28.9 us
  Pallas kernels  28.3 us (97%)
  between operations  0.64 us (2%)
    pallas_call x1, Pallas kernels, body(): pl.pallas_call(functools.partial(kernel, sizes), out_shape=(jax.ShapeDtyp...  26.3 us
    pallas_call x1, Pallas kernels, body(): pl.pallas_call(hand_over, out_shape=(jax.ShapeDtypeStruct(density.shape,...  1.95 us

profile of v6, /device:TPU:12, one launch (start us, length us, event | category | flops | bytes accessed | tf_op | source)
XLA Modules:
  0.0 28.9 jit_solution(12794183004222356242)
XLA Ops:
  0.6 26.3 %shard_map.95 = (f32[1024,128]{1,0:T(8,128)}, f32[4,96,128]{2,1,0:T(8,128)}) custom-call(f32[1024,128]{1,0:T(8,128)} %bitcast.11, f32[16,128]{1,0:T(8,128)} %bitcast.13, f32[1,64]{1,0:T(1,128)} %bitcast.14, f32[1,64]{1,0:T(1,128)} %bitcast.15, f32[64,96]{1,0:T(8,128)} %bitcast.12, s32[7]{0:T(128)} %bitcast.16, s32[7]{0:T(128)} %bitcast.17, ...), custom_call_target="tpu_custom_call" | custom-call | tf_op jit(solution)/shard_map/pallas_call | solution.py:337
  27.0 2.0 %shard_map.96 = (f32[1024,128]{1,0:T(8,128)}, f32[4,96,128]{2,1,0:T(8,128)}) custom-call(f32[1024,128]{1,0:T(8,128)} %get-tuple-element.6.density_in, f32[4,96,128]{2,1,0:T(8,128)} %get-tuple-element.7.sky_in), custom_call_target="tpu_custom_call" | custom-call | tf_op jit(solution)/shard_map/pallas_call | solution.py:389
